TPU v7x, 32 devices: a whole 2x2x4 slice. The times are simulated.
32 devices in a mesh: groups: 2 (over x), dom: 16 (over z, y, core).
Axes of the slice: x: 2, y: 2, z: 4, core: 2. Of those that a mesh axis runs over, the one named last changes fastest.
Arguments:
- source: bfloat16 [72, 262144], P(None, ('groups', 'dom')), parts along dimension 1, may hold values from -6 to 6
- tile_weight: bfloat16 [8192, 128, 128], P('dom'), may hold values from -0.0625 to 0.0625
- tile_source: int32 [8192], P('dom'), may hold values from 0 to 127
- tile_slot: int32 [8192], P('dom'), may hold values from 0 to 15
- tile_count: int32 [16], P('dom'), may hold values from 64 to 512, as said below
- dest_block: int32 [256], P('dom'), may hold values from 0 to 63, as said below
- embed_weight: bfloat16 [1152, 1024], replicated, may hold values from -0.1875 to 0.1875
- embed_bias: float32 [1024], replicated, may hold values from -3 to 3
Outputs:
- remapped: bfloat16 [128, 72, 128], P(('groups', 'dom')), parts along dimension 0
- embedded: bfloat16 [1024, 1024], P(('groups', 'dom')), parts along dimension 0
There are 2 independent parts, one for each index of `groups`. A program takes and returns all parts, laid end to end along the dimension named above; an argument that names none is the same for every part. Nothing has to cross between parts.
Inputs may be any that keep to these rules, and one draw needn't show every extreme that they name: `tile_count`: number of live tiles of each device; the later tile slots are unused. Some device has all 512 tiles live. `dest_block`: the owner of target block b is device b // 4. Within one device's 16 entries the blocks are distinct and at most 2 of them belong to any one owner; on every device some owner has exactly 2.
All inputs are finite; a program needn't handle non-finite values.
Results may differ from a plain program's by a relative error of at most 0.0046.
Values may be sent and summed in bfloat16 or wider, within the bound.
No kernel may reach another device: no remote copies, remote signals or barrier semaphores. Data moves between devices by JAX's collectives and lax.ppermute only.
A program may use at most 128 MiB of HBM per device.

v0:
```python
import jax
import jax.numpy as jnp
from jax import lax
from jax.sharding import PartitionSpec as P

PATCH = 4
CAP = 2
TB_DEV = 4


def extended_2(cells, sides, width):
    for axis, dim in sides:
        count = lax.axis_size(axis)
        head = lax.slice_in_dim(cells, 0, width, axis=dim)
        tail = lax.slice_in_dim(cells, cells.shape[dim] - width, cells.shape[dim], axis=dim)
        cells = jnp.concatenate(
            [
                lax.ppermute(tail, axis, [(i, (i + 1) % count) for i in range(count)]),
                cells,
                lax.ppermute(head, axis, [((i + 1) % count, i) for i in range(count)]),
            ],
            axis=dim,
        )
    return cells


def local(
    source, tile_weight, tile_source, tile_slot, tile_count, dest_block, embed_weight, embed_bias
):
    channels, own_cells = source.shape
    block_size = tile_weight.shape[1]
    own_blocks = own_cells // block_size
    rim_blocks = own_blocks // 2
    ext_count = own_blocks + 2 * rim_blocks
    tile_total = tile_weight.shape[0]
    slot_total = dest_block.shape[0]
    group_size = 128
    extended = extended_2(source, (("dom", 1),), rim_blocks * block_size)
    ext_blocks = extended.reshape(channels, ext_count, block_size)
    live_total = tile_count[0]
    slot_ids = jnp.arange(slot_total, dtype=jnp.int32)
    block_ids = jnp.arange(ext_count, dtype=jnp.int32)

    def add_group(group, totals):
        first = group * group_size
        indices = lax.dynamic_slice_in_dim(tile_source, first, group_size)
        choose = (indices[:, None] == block_ids[None, :]).astype(jnp.bfloat16)
        picked = jnp.einsum(
            "gb,cbi->cgi", choose, ext_blocks, preferred_element_type=jnp.float32
        ).astype(jnp.bfloat16)
        weights = lax.dynamic_slice_in_dim(tile_weight, first, group_size, 0)
        products = jnp.einsum("cgi,gij->gcj", picked, weights, preferred_element_type=jnp.float32)
        active = first + jnp.arange(group_size, dtype=jnp.int32) < live_total
        targets = lax.dynamic_slice_in_dim(tile_slot, first, group_size)
        placing = ((slot_ids[:, None] == targets[None, :]) & active[None, :]).astype(jnp.float32)
        return totals + jnp.einsum(
            "sg,gcj->scj", placing, products, precision=lax.Precision.HIGHEST
        )

    group_count = tile_total // group_size
    combined = lax.fori_loop(
        0, group_count, add_group, jnp.zeros((slot_total, channels, block_size), jnp.float32)
    )
    peers = lax.axis_size("dom")
    owners = dest_block // TB_DEV
    local_rows = dest_block % TB_DEV
    earlier = (owners[None, :] == owners[:, None]) & (slot_ids[None, :] < slot_ids[:, None])
    position = owners * CAP + jnp.sum(earlier.astype(jnp.int32), axis=1)
    buffer_rows = jnp.arange(peers * CAP, dtype=jnp.int32)
    placing = position[None, :] == buffer_rows[:, None]
    outgoing = jnp.einsum(
        "bs,scj->bcj", placing.astype(jnp.float32), combined, precision=lax.Precision.HIGHEST
    )
    labels = jnp.sum(jnp.where(placing, local_rows[None, :] + 1, 0), axis=1) - 1
    incoming, arrived = (
        lax.all_to_all(outgoing, "dom", split_axis=0, concat_axis=0, tiled=True),
        lax.all_to_all(labels, "dom", split_axis=0, concat_axis=0, tiled=True),
    )
    owned_rows = jnp.arange(TB_DEV, dtype=jnp.int32)
    collect = (arrived[None, :] == owned_rows[:, None]).astype(jnp.float32)
    summed = jnp.einsum("kb,bcj->kcj", collect, incoming, precision=lax.Precision.HIGHEST)
    remapped = summed.astype(jnp.bfloat16)
    per_block = block_size // (PATCH * PATCH)
    patches = remapped.reshape(TB_DEV, channels, PATCH, per_block, PATCH)
    patches = patches.transpose(0, 3, 1, 2, 4).reshape(TB_DEV * per_block, channels * PATCH * PATCH)
    embedded = jnp.dot(patches, embed_weight, preferred_element_type=jnp.float32) + embed_bias
    return (remapped, embedded.astype(jnp.bfloat16))


def solution(mesh):
    placed = (
        P(None, ("groups", "dom")),
        P("dom", None, None),
        P("dom"),
        P("dom"),
        P("dom"),
        P("dom"),
        P(),
        P(),
    )
    return jax.shard_map(
        local,
        mesh=mesh,
        in_specs=placed,
        out_specs=(P(("groups", "dom"), None, None), P(("groups", "dom"), None)),
        check_vma=False,
    )
```

profile of v0, /device:TPU:13, one launch (start us, length us, event | category | flops | bytes accessed | tf_op | source)
XLA Modules:
  0.0 132.9 jit_solution(14130334814147793098)
XLA Ops:
  0.7 2.5 %fusion.36 = (bf16[72,4096]{1,0:T(8,128)(2,1)}, bf16[72,4096]{1,0:T(8,128)(2,1)}) fusion(bf16[72,8192]{1,0:T(8,128)(2,1)} %param.10), kind=kLoop, calls=%fused_computation.44 | loop fusion | bytes 2359296 | tf_op jit(solution)/shard_map/slice | solution.py:15
  3.8 2.0 %collective-permute-start = (bf16[72,4096]{1,0:T(8,128)(2,1)}, bf16[72,4096]{1,0:T(8,128)(2,1)}, u32[]{:S(2)}, u32[]{:S(2)}) collective-permute-start(bf16[72,4096]{1,0:T(8,128)(2,1)} %get-tuple-element.207), channel_id=1, source_target_pairs={{0,1},{1,2},{2,3},{3,4},{4,5},{5,6},{6,7},{7,8},{8,9},{9,10},{10,1... | collective-permute-start | bytes 1769480 | tf_op jit(solution)/shard_map/ppermute | solution.py:18
  6.8 7.8 %all-to-all-start = ((s32[16,2,1]{1,2,0:T(1,128)}), s32[16,2,1]{1,2,0:T(1,128)S(1)}, u32[]{:S(2)}, u32[]{:S(2)}) async-start(s32[16,2,1]{1,2,0:T(1,128)} %bitcast), calls=%async_computation | async-start | bytes 16384 | tf_op jit(solution)/shard_map/all_to_all | solution.py:77
  14.6 1.6 %maximum_bitcast_fusion = bf16[9,8,128,128]{3,1,2,0:T(8,128)(2,1)S(1)} fusion(bf16[72,4096]{1,0:T(8,128)(2,1)S(1)} %collective-permute-done.1, bf16[72,8192]{1,0:T(8,128)(2,1)} %param.10, bf16[72,4096]{1,0:T(8,128)(2,1)} %collective-permute-done), kind=kLoop, calls=%fused_computation.19 | loop fusion | flops 7077888 | bytes 4718592
  16.2 2.1 %copy.30 = bf16[9,8,128,128]{3,2,1,0:T(8,128)(2,1)} copy(bf16[9,8,128,128]{3,1,2,0:T(8,128)(2,1)S(1)} %maximum_bitcast_fusion) | data formatting | bytes 4718592
  18.3 63.4 %while.14 = (s32[]{:T(128)}, f32[16,72,128]{2,0,1:T(8,128)S(1)}, s32[512]{0:T(512)}, s32[]{:T(128)}, s32[512]{0:T(512)}, /*index=5*/bf16[72,128,128]{2,1,0:T(8,1...) while((s32[]{:T(128)}, f32[16,72,128]{2,0,1:T(8,128)S(1)}, ...), condition=%wide.region_3.4_spmd.clone, body=%wide.region_2.3_spmd.clone.sunk | while | flops 831967488 | bytes 21892544 | solution.py:61
  18.3 0.8 dynamic_slice.30
  19.1 2.5 %convert_bitcast_fusion.2 = bf16[72,128,128]{2,1,0:T(8,128)(2,1)S(1)} fusion(bf16[72,128,128]{2,1,0:T(8,128)(2,1)} %get-tuple-element.281, s32[128]{0:T(128)S(1)} %dynamic_slice.30), kind=kOutput, calls=%fused_computation.7.clone.1 | convolution fusion | flops 303185920 | bytes 4719104 | tf_op jit(solution)/shard_map/while/body/eval_jaxpr/gb,cbi->cgi/dot_general | solution.py:48
  21.6 6.9 %fusion.55 = f32[128,72,128]{2,1,0:T(8,128)} fusion(bf16[512,128,128]{2,1,0:T(8,128)(2,1)} %get-tuple-element.282, s32[]{:T(128)S(6)} %select_n.35, bf16[72,128,128]{2,1,0:T(8,128)(2,1)S(1)} %convert_bitcast_fusion.2), kind=kOutput, calls=%fused_computation.4.clone.1 | convolution fusion | flops 301989888 | bytes 11272196 | tf_op jit(solution)/shard_map/while/body/eval_jaxpr/cgi,gij->gcj/dot_general | solution.py:52
  28.4 0.8 dynamic_slice.31
  29.9 4.3 %fusion.56 = f32[16,72,128]{2,0,1:T(8,128)S(1)} fusion(f32[128,72,128]{2,1,0:T(8,128)} %fusion.55, f32[16,72,128]{2,0,1:T(8,128)S(1)} %get-tuple-element.266, pred[]{:T(512)S(6)} %compare.6, s32[128]{0:T(128)S(1)} %dynamic_slice.31, pred[128]{0:T(512)(128)(4,1)S(1)} %add_compare_fusion.2), kind=kOutput, calls=%fused_computation.8.clone.1 | convolution fusion | flops 226791424 | bytes 5898881 | tf_op jit(solution)/shard_map/while/body/eval_jaxpr/sg,gcj->scj/dot_general | solution.py:56
  34.2 0.8 dynamic_slice.30
  34.9 2.5 %convert_bitcast_fusion.2 = bf16[72,128,128]{2,1,0:T(8,128)(2,1)S(1)} fusion(bf16[72,128,128]{2,1,0:T(8,128)(2,1)} %get-tuple-element.281, s32[128]{0:T(128)S(1)} %dynamic_slice.30), kind=kOutput, calls=%fused_computation.7.clone.1 | convolution fusion | flops 303185920 | bytes 4719104 | tf_op jit(solution)/shard_map/while/body/eval_jaxpr/gb,cbi->cgi/dot_general | solution.py:48
  37.4 6.9 %fusion.55 = f32[128,72,128]{2,1,0:T(8,128)} fusion(bf16[512,128,128]{2,1,0:T(8,128)(2,1)} %get-tuple-element.282, s32[]{:T(128)S(6)} %select_n.35, bf16[72,128,128]{2,1,0:T(8,128)(2,1)S(1)} %convert_bitcast_fusion.2), kind=kOutput, calls=%fused_computation.4.clone.1 | convolution fusion | flops 301989888 | bytes 11272196 | tf_op jit(solution)/shard_map/while/body/eval_jaxpr/cgi,gij->gcj/dot_general | solution.py:52
  44.3 0.8 dynamic_slice.31
  45.7 4.3 %fusion.56 = f32[16,72,128]{2,0,1:T(8,128)S(1)} fusion(f32[128,72,128]{2,1,0:T(8,128)} %fusion.55, f32[16,72,128]{2,0,1:T(8,128)S(1)} %get-tuple-element.266, pred[]{:T(512)S(6)} %compare.6, s32[128]{0:T(128)S(1)} %dynamic_slice.31, pred[128]{0:T(512)(128)(4,1)S(1)} %add_compare_fusion.2), kind=kOutput, calls=%fused_computation.8.clone.1 | convolution fusion | flops 226791424 | bytes 5898881 | tf_op jit(solution)/shard_map/while/body/eval_jaxpr/sg,gcj->scj/dot_general | solution.py:56
  50.0 0.8 dynamic_slice.30
  50.8 2.5 %convert_bitcast_fusion.2 = bf16[72,128,128]{2,1,0:T(8,128)(2,1)S(1)} fusion(bf16[72,128,128]{2,1,0:T(8,128)(2,1)} %get-tuple-element.281, s32[128]{0:T(128)S(1)} %dynamic_slice.30), kind=kOutput, calls=%fused_computation.7.clone.1 | convolution fusion | flops 303185920 | bytes 4719104 | tf_op jit(solution)/shard_map/while/body/eval_jaxpr/gb,cbi->cgi/dot_general | solution.py:48
  53.3 6.9 %fusion.55 = f32[128,72,128]{2,1,0:T(8,128)} fusion(bf16[512,128,128]{2,1,0:T(8,128)(2,1)} %get-tuple-element.282, s32[]{:T(128)S(6)} %select_n.35, bf16[72,128,128]{2,1,0:T(8,128)(2,1)S(1)} %convert_bitcast_fusion.2), kind=kOutput, calls=%fused_computation.4.clone.1 | convolution fusion | flops 301989888 | bytes 11272196 | tf_op jit(solution)/shard_map/while/body/eval_jaxpr/cgi,gij->gcj/dot_general | solution.py:52
  60.2 0.8 dynamic_slice.31
  61.6 4.3 %fusion.56 = f32[16,72,128]{2,0,1:T(8,128)S(1)} fusion(f32[128,72,128]{2,1,0:T(8,128)} %fusion.55, f32[16,72,128]{2,0,1:T(8,128)S(1)} %get-tuple-element.266, pred[]{:T(512)S(6)} %compare.6, s32[128]{0:T(128)S(1)} %dynamic_slice.31, pred[128]{0:T(512)(128)(4,1)S(1)} %add_compare_fusion.2), kind=kOutput, calls=%fused_computation.8.clone.1 | convolution fusion | flops 226791424 | bytes 5898881 | tf_op jit(solution)/shard_map/while/body/eval_jaxpr/sg,gcj->scj/dot_general | solution.py:56
  65.9 0.8 dynamic_slice.30
  66.7 2.5 %convert_bitcast_fusion.2 = bf16[72,128,128]{2,1,0:T(8,128)(2,1)S(1)} fusion(bf16[72,128,128]{2,1,0:T(8,128)(2,1)} %get-tuple-element.281, s32[128]{0:T(128)S(1)} %dynamic_slice.30), kind=kOutput, calls=%fused_computation.7.clone.1 | convolution fusion | flops 303185920 | bytes 4719104 | tf_op jit(solution)/shard_map/while/body/eval_jaxpr/gb,cbi->cgi/dot_general | solution.py:48
  69.1 6.9 %fusion.55 = f32[128,72,128]{2,1,0:T(8,128)} fusion(bf16[512,128,128]{2,1,0:T(8,128)(2,1)} %get-tuple-element.282, s32[]{:T(128)S(6)} %select_n.35, bf16[72,128,128]{2,1,0:T(8,128)(2,1)S(1)} %convert_bitcast_fusion.2), kind=kOutput, calls=%fused_computation.4.clone.1 | convolution fusion | flops 301989888 | bytes 11272196 | tf_op jit(solution)/shard_map/while/body/eval_jaxpr/cgi,gij->gcj/dot_general | solution.py:52
  77.4 4.3 %fusion.56 = f32[16,72,128]{2,0,1:T(8,128)S(1)} fusion(f32[128,72,128]{2,1,0:T(8,128)} %fusion.55, f32[16,72,128]{2,0,1:T(8,128)S(1)} %get-tuple-element.266, pred[]{:T(512)S(6)} %compare.6, s32[128]{0:T(128)S(1)} %dynamic_slice.31, pred[128]{0:T(512)(128)(4,1)S(1)} %add_compare_fusion.2), kind=kOutput, calls=%fused_computation.8.clone.1 | convolution fusion | flops 226791424 | bytes 5898881 | tf_op jit(solution)/shard_map/while/body/eval_jaxpr/sg,gcj->scj/dot_general | solution.py:56
  82.5 1.7 %copy.25 = f32[32,72,128]{2,1,0:T(8,128)} copy(f32[32,72,128]{2,0,1:T(8,128)S(1)} %fusion.29) | data formatting | bytes 2359296 | tf_op jit(solution)/shard_map/bs,scj->bcj/dot_general | solution.py:71
  84.2 11.1 %all-to-all-start.1 = ((f32[32,72,128]{2,1,0:T(8,128)}), f32[32,72,128]{2,1,0:T(8,128)S(1)}, u32[]{:S(2)}, u32[]{:S(2)}) async-start(f32[32,72,128]{2,1,0:T(8,128)} %copy.25), calls=%async_computation.1 | async-start | bytes 2359296 | tf_op jit(solution)/shard_map/all_to_all | solution.py:76
  96.6 26.5 %all-to-all-done.1 = f32[32,72,128]{2,1,0:T(8,128)S(1)} async-done(((f32[32,72,128]{2,1,0:T(8,128)}), f32[32,72,128]{2,1,0:T(8,128)S(1)}, u32[]{:S(2)}, u32[]{:S(2)}) %all-to-all-start.1) | async-done | bytes 1179680 | tf_op jit(solution)/shard_map/all_to_all | solution.py:76
  124.9 1.6 %copy.27 = bf16[4,72,128]{1,2,0:T(8,128)(2,1)} copy(bf16[4,72,128]{2,0,1:T(4,128)(2,1)} %copy-done.1) | data formatting | bytes 147456 | tf_op jit(solution)/shard_map/convert_element_type | solution.py:82
  126.6 2.9 %copy.28 = bf16[4,8,72,4,4]{1,0,4,3,2:T(4,128)(2,1)S(1)} copy(bf16[4,8,72,4,4]{2,4,1,3,0:T(4,128)(2,1)} %bitcast.38) | data formatting | bytes 147456 | tf_op jit(solution)/shard_map/transpose | solution.py:85
  129.5 1.3 reshape.46
  130.8 2.1 %fusion.26 = bf16[32,1024]{1,0:T(8,128)(2,1)} fusion(bf16[32,1152]{0,1:T(8,128)(2,1)} %reshape.46, bf16[1152,1024]{1,0:T(8,128)(2,1)S(1)} %copy-done, f32[1024]{0:T(1024)S(1)} %copy-done.2), kind=kOutput, calls=%fused_computation.24 | convolution fusion | flops 75563008 | bytes 2502656 | tf_op jit(solution)/shard_map/dot_general | solution.py:86
  (30 shorter events, 8.9 us)
Async XLA Ops:
  0.6 130.2 %copy-start = (bf16[1152,1024]{1,0:T(8,128)(2,1)S(1)}, bf16[1152,1024]{1,0:T(8,128)(2,1)}, u32[]{:S(2)}) copy-start(bf16[1152,1024]{1,0:T(8,128)(2,1)} %param.16) | copy-start | bytes 7077892
  0.6 5.2 %copy-start.3 = (s32[16]{0:T(128)S(1)}, s32[16]{0:T(128)}, u32[]{:S(2)}) copy-start(s32[16]{0:T(128)} %param.15) | copy-start | bytes 196
  3.2 11.4 %collective-permute-start.1 = (bf16[72,4096]{1,0:T(8,128)(2,1)}, bf16[72,4096]{1,0:T(8,128)(2,1)S(1)}, u32[]{:S(2)}, u32[]{:S(2)}) collective-permute-start(bf16[72,4096]{1,0:T(8,128)(2,1)} %get-tuple-element.208), channel_id=1, source_target_pairs={{1,0},{2,1},{3,2},{4,3},{5,4},{6,5},{7,6},{8,7},{9,8},{10,9},{11,1... | collective-permute-start | bytes 1769480 | tf_op jit(solution)/shard_map/ppermute | solution.py:20
  3.8 10.8 %collective-permute-start = (bf16[72,4096]{1,0:T(8,128)(2,1)}, bf16[72,4096]{1,0:T(8,128)(2,1)}, u32[]{:S(2)}, u32[]{:S(2)}) collective-permute-start(bf16[72,4096]{1,0:T(8,128)(2,1)} %get-tuple-element.207), channel_id=1, source_target_pairs={{0,1},{1,2},{2,3},{3,4},{4,5},{5,6},{6,7},{7,8},{8,9},{9,10},{10,1... | collective-permute-start | bytes 1769480 | tf_op jit(solution)/shard_map/ppermute | solution.py:18
  6.8 77.4 %all-to-all-start = ((s32[16,2,1]{1,2,0:T(1,128)}), s32[16,2,1]{1,2,0:T(1,128)S(1)}, u32[]{:S(2)}, u32[]{:S(2)}) async-start(s32[16,2,1]{1,2,0:T(1,128)} %bitcast), calls=%async_computation | async-start | bytes 16384 | tf_op jit(solution)/shard_map/all_to_all | solution.py:77
  84.2 38.9 %all-to-all-start.1 = ((f32[32,72,128]{2,1,0:T(8,128)}), f32[32,72,128]{2,1,0:T(8,128)S(1)}, u32[]{:S(2)}, u32[]{:S(2)}) async-start(f32[32,72,128]{2,1,0:T(8,128)} %copy.25), calls=%async_computation.1 | async-start | bytes 2359296 | tf_op jit(solution)/shard_map/all_to_all | solution.py:76
  96.5 34.3 %copy-start.2 = (f32[1024]{0:T(1024)S(1)}, f32[1024]{0:T(1024)}, u32[]{:S(2)}) copy-start(f32[1024]{0:T(1024)} %param.17) | copy-start | bytes 12292
  123.7 0.6 copy-start.1
where the time goes:
time: 134 us; the launch traced here: 133 us
  matrix products  58.1 us (43%)
  waiting for transfers between devices  26.5 us (20%)
  starting transfers between devices  21.6 us (16%)
  local copies, waits for them, and re-layouts  20.8 us (16%)
  other arithmetic  5.14 us (4%)
    dot_general x4, matrix products, add_group(): jnp.einsum('cgi,gij->gcj', picked, weights, preferred_element_type=jnp.fl...  27.6 us
    all_to_all x1, waiting for transfers between devices, local(): lax.all_to_all(outgoing, 'dom', split_axis=0, concat_axis=0, tiled=True)  26.5 us
    dot_general x4, matrix products, add_group(): jnp.einsum('sg,gcj->scj', placing, products, precision=lax.Precision.HIGH...  17.2 us
    all_to_all x1, starting transfers between devices, local(): lax.all_to_all(outgoing, 'dom', split_axis=0, concat_axis=0, tiled=True)  11.1 us
    dot_general x4, matrix products, add_group(): jnp.einsum('gb,cbi->cgi', choose, ext_blocks, preferred_element_type=jnp....  9.92 us
    all_to_all x1, starting transfers between devices, local(): lax.all_to_all(labels, 'dom', split_axis=0, concat_axis=0, tiled=True)  7.79 us
    unnamed x10, local copies, waits for them, and re-layouts  3.39 us
    dynamic_slice x4, local copies, waits for them, and re-layouts, add_group(): indices = lax.dynamic_slice_in_dim(tile_source, first, group_size)  3.03 us
  transfers between devices with their start and end apart: 4, of which 1 were waited for; matrix products, arithmetic and copies ran while one was open for 54% of the time, Pallas kernels for 0%

commit v1 on v0

v1 whole, which is shorter than its diff:
```python
import functools

import jax
import jax.numpy as jnp
from jax import lax
from jax.experimental import pallas as pl
from jax.experimental.pallas import tpu as pltpu
from jax.sharding import PartitionSpec as P

PATCH = 4
CAP = 2
TB_DEV = 4
SEG = 4
UNROLL = 4
CHUNK = 64
VMEM = pl.BlockSpec(memory_space=pltpu.VMEM)
SMEM = pl.BlockSpec(memory_space=pltpu.SMEM)
ANY = pl.BlockSpec(memory_space=pl.ANY)


def bits_of(tiles):
    return tiles.bit_length()


def list_sizes(tiles, slots):
    step = SEG * UNROLL
    entries = -(-(tiles + slots * (SEG - 1)) // step) * step
    return entries, entries // SEG


def schedule(tile_source, tile_slot, live_total, slots, own, rim):
    tiles = tile_source.shape[0]
    entries, segments = list_sizes(tiles, slots)
    ids = jnp.arange(tiles, dtype=jnp.int32)
    inner = (tile_source >= rim) & (tile_source < rim + own)
    kind = jnp.where(inner, 0, 1)
    block = jnp.where(inner | (tile_source < rim), tile_source - jnp.where(inner, rim, 0), tile_source - own)
    code = (block << bits_of(tiles)) | (tiles - ids)
    bins = jnp.where(ids < live_total, kind * slots + tile_slot, -1)
    chosen = bins[:, None] == jnp.arange(2 * slots, dtype=jnp.int32)[None, :]
    before = (ids[None, :] < ids[:, None]).astype(jnp.bfloat16)
    rank = jnp.dot(before, chosen.astype(jnp.bfloat16), preferred_element_type=jnp.float32)
    total = jnp.sum(chosen.astype(jnp.int32), axis=0)
    length = (total + SEG - 1) // SEG
    slot_ids = jnp.arange(slots, dtype=jnp.int32)
    length = length.reshape(2, slots)
    ends = jnp.sum(jnp.where(slot_ids[None, :] <= slot_ids[:, None], length[:, None, :], 0), axis=2)
    begins = (ends - length).reshape(-1)
    place = jnp.sum(jnp.where(chosen, rank.astype(jnp.int32) + begins[None, :] * SEG, 0), axis=1)
    place = jnp.where(bins >= 0, place + jnp.where(bins >= slots, entries, 0), -1)
    spots = jnp.arange(2 * entries, dtype=jnp.int32)
    listed = jnp.sum(jnp.where(place[None, :] == spots[:, None], code[None, :], 0), axis=1)
    segment_ids = jnp.arange(segments, dtype=jnp.int32)
    owner = jnp.sum((ends[:, None, :] <= segment_ids[None, :, None]).astype(jnp.int32), axis=2)
    owner = jnp.minimum(owner, slots - 1)
    return jnp.concatenate([listed, owner.reshape(-1), ends[:, slots - 1]])


def run_segments(kind, tiles, slots, meta, x, w, acc):
    entries, segments = list_sizes(tiles, slots)
    bits = bits_of(tiles)
    total = meta[2 * entries + 2 * segments + kind]

    def step(i, carry):
        results = []
        for u in range(UNROLL):
            first = kind * entries + (i * UNROLL + u) * SEG
            xs, ws = [], []
            for k in range(SEG):
                code = meta[first + k]
                column = pl.multiple_of((code >> bits) * 128, 128)
                xs.append(x[:, pl.ds(column, 128)])
                ws.append(w[tiles - (code & ((1 << bits) - 1))])
            results.append(
                jnp.dot(
                    jnp.concatenate(xs, axis=1),
                    jnp.concatenate(ws, axis=0),
                    preferred_element_type=jnp.float32,
                )
            )
        for u in range(UNROLL):
            slot = meta[2 * entries + kind * segments + i * UNROLL + u]
            acc[slot] += results[u]
        return carry

    lax.fori_loop(0, (total + UNROLL - 1) // UNROLL, step, 0)


def inner_kernel(tiles, slots, meta, count, source, weights, acc, held, sems):
    live = count[0]
    chunks = tiles // CHUNK

    def copy(c):
        part = pl.ds(c * CHUNK, CHUNK)
        return pltpu.make_async_copy(weights.at[part], held.at[part], sems.at[c])

    for c in range(chunks):
        pl.when(c * CHUNK < live)(lambda c=c: copy(c).start())
    acc[...] = jnp.zeros_like(acc)
    held[tiles] = jnp.zeros(held.shape[1:], held.dtype)
    for c in range(chunks):
        pl.when(c * CHUNK < live)(lambda c=c: copy(c).wait())
    run_segments(0, tiles, slots, meta, source, held, acc)


def halo_kernel(tiles, slots, meta, position, left, right, partial, held, out, x, acc, sems):
    rim = left.shape[1]
    copies = [
        pltpu.make_async_copy(left, x.at[:, pl.ds(0, rim)], sems.at[0]),
        pltpu.make_async_copy(right, x.at[:, pl.ds(rim, rim)], sems.at[1]),
    ]
    for c in copies:
        c.start()
    out[...] = jnp.zeros_like(out)
    acc[...] = partial[...]
    for c in copies:
        c.wait()
    run_segments(1, tiles, slots, meta, x, held, acc)

    def place(s, carry):
        out[position[s]] = acc[s].astype(out.dtype)
        return carry

    lax.fori_loop(0, slots, place, 0)


def final_kernel(labels, incoming, choose, weight, bias, remapped, embedded, acc, turned):
    acc[...] = jnp.zeros_like(acc)

    def add(r, carry):
        label = labels[r]

        @pl.when(label >= 0)
        def _():
            acc[label] += incoming[r].astype(jnp.float32)

        return carry

    lax.fori_loop(0, incoming.shape[0], add, 0)
    embed(acc, choose, weight, bias, remapped, embedded, turned)


def embed(acc, choose, weight, bias, remapped, embedded, turned):
    blocks, channels, cells = acc.shape
    for b in range(blocks):
        value = acc[b].astype(jnp.bfloat16)
        remapped[b] = value
        turned[b] = lax.dot_general(
            choose[...], value, (((1,), (1,)), ((), ())), preferred_element_type=jnp.float32
        )
    per_block = cells // (PATCH * PATCH)
    total = jnp.broadcast_to(bias[...], (blocks * per_block, bias.shape[1]))
    for s in range(PATCH * PATCH):
        rows = turned[:, s * per_block : (s + 1) * per_block, :]
        rows = rows.reshape(blocks * per_block, channels).astype(jnp.bfloat16)
        total = total + jnp.dot(rows, weight[s], preferred_element_type=jnp.float32)
    embedded[...] = total.astype(jnp.bfloat16)


def chooser(cells):
    per_block = cells // (PATCH * PATCH)
    row = jnp.arange(cells, dtype=jnp.int32)
    r, q, p = row // (PATCH * per_block), row // per_block % PATCH, row % per_block
    wanted = r * (PATCH * per_block) + p * PATCH + q
    return (wanted[:, None] == jnp.arange(cells, dtype=jnp.int32)[None, :]).astype(jnp.bfloat16)


def local(
    source, tile_weight, tile_source, tile_slot, tile_count, dest_block, embed_weight, embed_bias
):
    channels, own_cells = source.shape
    tiles, block_size, _ = tile_weight.shape
    own = own_cells // block_size
    rim = own // 2
    slots = dest_block.shape[0]
    peers = lax.axis_size("dom")
    width = rim * block_size
    emb = embed_weight.shape[1]

    head = lax.slice_in_dim(source, 0, width, axis=1)
    tail = lax.slice_in_dim(source, own_cells - width, own_cells, axis=1)
    left = lax.ppermute(tail, "dom", [(i, (i + 1) % peers) for i in range(peers)])
    right = lax.ppermute(head, "dom", [((i + 1) % peers, i) for i in range(peers)])

    meta = schedule(tile_source, tile_slot, tile_count[0], slots, own, rim)
    slot_ids = jnp.arange(slots, dtype=jnp.int32)
    owners = dest_block // TB_DEV
    earlier = (owners[None, :] == owners[:, None]) & (slot_ids[None, :] < slot_ids[:, None])
    position = owners * CAP + jnp.sum(earlier.astype(jnp.int32), axis=1)
    rows = jnp.arange(peers * CAP, dtype=jnp.int32)
    placing = position[None, :] == rows[:, None]
    labels = jnp.sum(jnp.where(placing, (dest_block % TB_DEV)[None, :] + 1, 0), axis=1) - 1
    arrived = lax.all_to_all(labels, "dom", split_axis=0, concat_axis=0, tiled=True)

    acc_shape = (slots, channels, block_size)
    held_shape = (tiles + 1, block_size, block_size)
    partial, held = pl.pallas_call(
        functools.partial(inner_kernel, tiles, slots),
        out_shape=(
            pltpu.VMEM(acc_shape, jnp.float32),
            pltpu.VMEM(held_shape, jnp.bfloat16),
        ),
        in_specs=[SMEM, SMEM, VMEM, ANY],
        out_specs=(VMEM, VMEM),
        scratch_shapes=[pltpu.SemaphoreType.DMA((tiles // CHUNK,))],
        compiler_params=pltpu.CompilerParams(vmem_limit_bytes=8 << 20),
        cost_estimate=pl.CostEstimate(
            flops=tiles * channels * block_size * block_size,
            bytes_accessed=tile_weight.size * 2,
            transcendentals=0,
        ),
        name="inner_tiles",
    )(meta, tile_count, source, pltpu.with_memory_space_constraint(tile_weight, pltpu.HBM))

    outgoing = pl.pallas_call(
        functools.partial(halo_kernel, tiles, slots),
        out_shape=jax.ShapeDtypeStruct((peers * CAP, channels, block_size), jnp.bfloat16),
        in_specs=[SMEM, SMEM, ANY, ANY, VMEM, VMEM],
        out_specs=VMEM,
        scratch_shapes=[
            pltpu.VMEM((channels, 2 * width), jnp.bfloat16),
            pltpu.VMEM(acc_shape, jnp.float32),
            pltpu.SemaphoreType.DMA((2,)),
        ],
        compiler_params=pltpu.CompilerParams(vmem_limit_bytes=16 << 20),
        cost_estimate=pl.CostEstimate(
            flops=tiles * channels * block_size * block_size,
            bytes_accessed=4 * channels * width * 2,
            transcendentals=0,
        ),
        name="halo_tiles",
    )(
        meta,
        position,
        left,
        right,
        pltpu.with_memory_space_constraint(partial, pltpu.VMEM),
        pltpu.with_memory_space_constraint(held, pltpu.VMEM),
    )

    incoming = lax.all_to_all(outgoing, "dom", split_axis=0, concat_axis=0, tiled=True)

    area = PATCH * PATCH
    weight = embed_weight.reshape(channels, area, emb).transpose(1, 0, 2)
    per_block = block_size // area
    return pl.pallas_call(
        final_kernel,
        out_shape=(
            jax.ShapeDtypeStruct((TB_DEV, channels, block_size), jnp.bfloat16),
            jax.ShapeDtypeStruct((TB_DEV * per_block, emb), jnp.bfloat16),
        ),
        in_specs=[SMEM, VMEM, VMEM, VMEM, VMEM],
        out_specs=(VMEM, VMEM),
        scratch_shapes=[
            pltpu.VMEM((TB_DEV, channels, block_size), jnp.float32),
            pltpu.VMEM((TB_DEV, block_size, channels), jnp.float32),
        ],
        compiler_params=pltpu.CompilerParams(vmem_limit_bytes=16 << 20),
        name="embed",
    )(arrived, incoming, chooser(block_size), weight, embed_bias.reshape(1, emb))


def solution(mesh):
    placed = (
        P(None, ("groups", "dom")),
        P("dom", None, None),
        P("dom"),
        P("dom"),
        P("dom"),
        P("dom"),
        P(),
        P(),
    )
    return jax.shard_map(
        local,
        mesh=mesh,
        in_specs=placed,
        out_specs=(P(("groups", "dom"), None, None), P(("groups", "dom"), None)),
        check_vma=False,
    )
```

time: 134 us -> 67.7 us (0.51)
  the two profiles are of different devices: /device:TPU:13 before, /device:TPU:0 now
where the time goes in v1:
time: 67.7 us; the launch traced here: 67.5 us
  Pallas kernels  19.8 us (29%)
  starting transfers between devices  15.5 us (23%)
  local copies, waits for them, and re-layouts  11.2 us (17%)
  waiting for transfers between devices  10.5 us (16%)
  other arithmetic  8.11 us (12%)
  between operations  1.44 us (2%)
  matrix products  0.94 us (1%)
    pallas_call x1, Pallas kernels, local(): pl.pallas_call(functools.partial(inner_kernel, tiles, slots), out_shape=(...  11.5 us
    all_to_all x1, waiting for transfers between devices, local(): lax.all_to_all(outgoing, 'dom', split_axis=0, concat_axis=0, tiled=True)  10.5 us
    all_to_all x1, starting transfers between devices, local(): lax.all_to_all(labels, 'dom', split_axis=0, concat_axis=0, tiled=True)  7.44 us
    pallas_call x1, Pallas kernels, local(): pl.pallas_call(functools.partial(halo_kernel, tiles, slots), out_shape=ja...  5.95 us
    ppermute x1, starting transfers between devices, local(): lax.ppermute(head, 'dom', [((i + 1) % peers, i) for i in range(peers)])  4.09 us
    all_to_all x1, starting transfers between devices, local(): lax.all_to_all(outgoing, 'dom', split_axis=0, concat_axis=0, tiled=True)  3.59 us
    reshape x1, local copies, waits for them, and re-layouts, local(): weight = embed_weight.reshape(channels, area, emb).transpose(1, 0, 2)  2.97 us
    pallas_call x1, Pallas kernels, local(): pl.pallas_call(final_kernel, out_shape=(jax.ShapeDtypeStruct((TB_DEV, cha...  2.38 us
  transfers between devices with their start and end apart: 4, of which 1 were waited for; matrix products, arithmetic and copies ran while one was open for 26% of the time, Pallas kernels for 26%

profile of v1, /device:TPU:0, one launch (start us, length us, event | category | flops | bytes accessed | tf_op | source)
XLA Modules:
  0.0 67.5 jit_solution(14733337555291360933)
XLA Ops:
  0.6 0.8 %and_select_fusion.7 = (s32[16]{0:T(128)S(1)}, s32[16]{0:T(128)S(1)}) fusion(s32[16]{0:T(128)} %param.13), kind=kLoop, calls=%fused_computation.36 | loop fusion | flops 320 | bytes 192 | tf_op jit(solution)/shard_map/jit(floor_divide)/jit(_where)/select_n | solution.py:187
  1.4 0.2 convert_reduce_fusion.2
  1.6 0.1 select_reduce_fusion.2
  1.7 0.7 %sub.59 = s32[16,2,1]{1,0,2:T(8,128)} reshape(s32[32]{0:T(128)S(1)} %broadcast_add_fusion.1) | data formatting | bytes 256 | tf_op jit(solution)/shard_map/sub | solution.py:192
  2.4 7.4 %all-to-all-start = ((s32[16,2,1]{1,2,0:T(1,128)}), s32[16,2,1]{1,2,0:T(1,128)}, u32[]{:S(2)}, u32[]{:S(2)}) async-start(s32[16,2,1]{1,2,0:T(1,128)} %bitcast), calls=%async_computation | async-start | bytes 16384 | tf_op jit(solution)/shard_map/all_to_all | solution.py:193
  9.9 1.3 %fusion.12 = (bf16[72,4096]{1,0:T(8,128)(2,1)S(1)}, bf16[72,4096]{1,0:T(8,128)(2,1)S(1)}) fusion(bf16[72,8192]{1,0:T(8,128)(2,1)} %source.1), kind=kLoop, calls=%fused_computation.63 | loop fusion | bytes 2359296 | tf_op jit(solution)/shard_map/slice | solution.py:180
  11.2 0.4 collective-permute-start
  11.6 4.1 %collective-permute-start.1 = (bf16[72,4096]{1,0:T(8,128)(2,1)S(1)}, bf16[72,4096]{1,0:T(8,128)(2,1)S(1)}, u32[]{:S(2)}, u32[]{:S(2)}) collective-permute-start(bf16[72,4096]{1,0:T(8,128)(2,1)S(1)} %get-tuple-element.6), channel_id=1, source_target_pairs={{1,0},{2,1},{3,2},{4,3},{5,4},{6,5},{7,6},{8,7},{9,8},{10,9},{11,1... | collective-permute-start | bytes 1769480 | tf_op jit(solution)/shard_map/ppermute | solution.py:183
  16.4 0.1 convert_reduce_fusion
  16.5 0.5 copy-done.4
  17.0 0.6 broadcast_add_fusion
  17.6 1.3 %sub.62 = s32[2,16]{1,0:T(2,128)} reshape(s32[32]{0:T(128)} %broadcast_add_fusion) | data formatting | bytes 256 | tf_op jit(solution)/shard_map/sub | solution.py:44
  18.9 0.7 %and_select_fusion.5 = s32[2,16]{1,0:T(2,128)S(1)} fusion(s32[2,16]{1,0:T(2,128)} %sub.62), kind=kLoop, calls=%fused_computation.33 | loop fusion | flops 480 | bytes 256 | tf_op jit(solution)/shard_map/jit(floor_divide)/jit(_where)/select_n | solution.py:44
  19.6 0.7 %select_reduce_fusion.1 = s32[2,16]{1,0:T(2,128)} fusion(s32[2,16]{1,0:T(2,128)S(1)} %and_select_fusion.5, pred[16,16]{1,0:T(8,128)(4,1)S(1)} %iota_compare_fusion.7), kind=kLoop, calls=%fused_computation.15 | loop fusion | flops 992 | bytes 512 | tf_op jit(solution)/shard_map/reduce_sum | solution.py:47
  20.3 0.8 %reduce_sum.69 = s32[32]{0:T(128)S(1)} reshape(s32[2,16]{1,0:T(2,128)} %select_reduce_fusion.1) | data formatting | bytes 256 | tf_op jit(solution)/shard_map/reduce_sum | solution.py:47
  21.1 0.8 %convert_reduce_fusion.1 = s32[2,140]{1,0:T(2,128)S(1)} fusion(s32[2,16]{1,0:T(2,128)} %select_reduce_fusion.1), kind=kLoop, calls=%fused_computation.12 | loop fusion | flops 13160 | bytes 1248 | tf_op jit(solution)/shard_map/reduce_sum | solution.py:54
  21.9 1.2 %subtract_multiply_fusion = s32[32]{0:T(128)} fusion(s32[32]{0:T(128)S(1)} %reduce_sum.69, s32[32]{0:T(128)} %copy-done.4), kind=kLoop, calls=%fused_computation.59 | loop fusion | flops 576 | bytes 384 | tf_op jit(solution)/shard_map/mul | solution.py:49
  23.1 0.6 broadcast_minimum_fusion
  23.7 1.4 %slice_reduce_fusion = s32[2]{0:T(128)} fusion(s32[2,16]{1,0:T(2,128)} %select_reduce_fusion.1), kind=kLoop, calls=%fused_computation.51 | loop fusion | bytes 16 | tf_op jit(solution)/shard_map/slice | solution.py:56
  25.1 0.8 %min.12 = s32[280]{0:T(512)S(1)} reshape(s32[2,140]{1,0:T(2,128)} %broadcast_minimum_fusion) | data formatting | bytes 2240 | tf_op jit(solution)/shard_map/min | solution.py:55
  25.8 0.9 %fusion.2 = s32[512]{0:T(512)S(1)} fusion(s32[32]{0:T(128)} %subtract_multiply_fusion, s32[512]{0:T(512)S(1)} %get-tuple-element.8), kind=kOutput, calls=%fused_computation.6 | convolution fusion | flops 17137152 | bytes 4224 | tf_op jit(solution)/shard_map/dot_general | solution.py:42
  26.8 0.9 %select_reduce_fusion = s32[1120]{0:T(1024)} fusion(s32[512]{0:T(512)S(1)} %get-tuple-element.9, s32[512]{0:T(512)S(1)} %add_select_fusion), kind=kLoop, calls=%fused_computation.1 | loop fusion | flops 1719200 | bytes 8576 | tf_op jit(solution)/shard_map/reduce_sum | solution.py:52
  27.7 0.8 %concatenate.3.meta = s32[1402]{0:T(1024)S(1)} concatenate(s32[1120]{0:T(1024)} %select_reduce_fusion, s32[280]{0:T(512)S(1)} %min.12, s32[2]{0:T(128)} %slice_reduce_fusion), dimensions={0} | concatenate | bytes 11216 | tf_op jit(solution)/shard_map/concatenate | solution.py:56
  28.5 11.5 %inner_tiles.1 = (f32[16,72,128]{2,1,0:T(8,128)S(1)}, bf16[513,128,128]{2,1,0:T(8,128)(2,1)S(1)}) custom-call(s32[1402]{0:T(1024)S(1)} %concatenate.3.meta, s32[1]{0:T(128)} %copy.25.count, bf16[72,8192]{1,0:T(8,128)(2,1)S(1)} %copy-done, bf16[512,128,128]{2,1,0:T(8,128)(2,1)} %weights.1), custom_call_target="tpu_custom_call" | custom-call | flops 603979776 | bytes 16777216 | tf_op jit(solution)/shard_map/inner_tiles/pallas_call | solution.py:197
  40.0 5.9 %halo_tiles.1 = bf16[32,72,128]{2,1,0:T(8,128)(2,1)} custom-call(s32[1402]{0:T(1024)S(1)} %concatenate.3.meta, s32[16]{0:T(128)S(1)} %multiply_add_fusion.position, bf16[72,4096]{1,0:T(8,128)(2,1)S(1)} %collective-permute-done.left, bf16[72,4096]{1,0:T(8,128)(2,1)S(1)} %collective-permute-done.1.right, f32[16,72,128]{2,1,0:T(8,128)S(1)} %get-tuple-element.4.partial, ...), custom_call_target="tpu_custom_call" | custom-call | flops 603979776 | bytes 2359296 | tf_op jit(solution)/shard_map/halo_tiles/pallas_call | solution.py:215
  46.0 3.6 %all-to-all-start.1 = ((bf16[32,72,128]{2,1,0:T(8,128)(2,1)}), bf16[32,72,128]{2,1,0:T(8,128)(2,1)S(1)}, u32[]{:S(2)}, u32[]{:S(2)}) async-start(bf16[32,72,128]{2,1,0:T(8,128)(2,1)} %halo_tiles.1), calls=%async_computation.1 | async-start | bytes 1179648 | tf_op jit(solution)/shard_map/all_to_all | solution.py:241
  49.6 3.0 %copy.24 = bf16[72,16,1024]{2,0,1:T(8,128)(2,1)S(1)} copy(bf16[72,16,1024]{2,1,0:T(8,128)(2,1)} %bitcast.11) | data formatting | bytes 4718592 | tf_op jit(solution)/shard_map/reshape | solution.py:244
  52.7 0.5 broadcast.302
  53.2 1.4 %reduce.5 = s32[16,2]{1,0:T(8,128)S(1)} reduce(s32[16,2,1]{1,2,0:T(1,128)} %all-to-all-done, s32[]{:T(128)} %broadcast.302), dimensions={2}, to_apply=%all_to_all.8.reduce_sub_computation.3 | reduce | bytes 260 | tf_op jit(solution)/shard_map/all_to_all | solution.py:193
  54.6 0.1 all_to_all.9.labels
  54.6 10.5 %all-to-all-done.1.incoming = bf16[32,72,128]{2,1,0:T(8,128)(2,1)S(1)} async-done(((bf16[32,72,128]{2,1,0:T(8,128)(2,1)}), bf16[32,72,128]{2,1,0:T(8,128)(2,1)S(1)}, u32[]{:S(2)}, u32[]{:S(2)}) %all-to-all-start.1) | async-done | bytes 589856 | tf_op jit(solution)/shard_map/all_to_all | solution.py:241
  65.1 2.4 %embed.1 = (bf16[4,72,128]{2,1,0:T(8,128)(2,1)}, bf16[32,1024]{1,0:T(8,128)(2,1)}) custom-call(s32[32]{0:T(128)S(1)} %all_to_all.9.labels, bf16[32,72,128]{2,1,0:T(8,128)(2,1)S(1)} %all-to-all-done.1.incoming, bf16[128,128]{1,0:T(8,128)(2,1)S(1)} %fusion.3.choose, bf16[16,72,1024]{2,1,0:T(8,128)(2,1)S(1)} %bitcast.9, f32[1,1024]{1,0:T(1,128)S(1)} %bitcast.10), custom_call_target="tpu_custom_call" | custom-call | tf_op jit(solution)/shard_map/embed/pallas_call | solution.py:246
  (19 shorter events, 0.2 us)
Async XLA Ops:
  0.6 27.9 %copy-start = (bf16[72,8192]{1,0:T(8,128)(2,1)S(1)}, bf16[72,8192]{1,0:T(8,128)(2,1)}, u32[]{:S(2)}) copy-start(bf16[72,8192]{1,0:T(8,128)(2,1)} %source.1) | copy-start | bytes 3538948
  2.4 43.6 %all-to-all-start = ((s32[16,2,1]{1,2,0:T(1,128)}), s32[16,2,1]{1,2,0:T(1,128)}, u32[]{:S(2)}, u32[]{:S(2)}) async-start(s32[16,2,1]{1,2,0:T(1,128)} %bitcast), calls=%async_computation | async-start | bytes 16384 | tf_op jit(solution)/shard_map/all_to_all | solution.py:193
  9.8 6.5 %copy-start.2 = (s32[512]{0:T(512)S(1)}, s32[512]{0:T(512)}, u32[]{:S(2)}) copy-start(s32[512]{0:T(512)} %param.11) | copy-start | bytes 6148
  9.8 6.5 %copy-start.3 = (s32[512]{0:T(512)S(1)}, s32[512]{0:T(512)}, u32[]{:S(2)}) copy-start(s32[512]{0:T(512)} %param.10) | copy-start | bytes 6148
  11.2 28.8 %collective-permute-start = (bf16[72,4096]{1,0:T(8,128)(2,1)S(1)}, bf16[72,4096]{1,0:T(8,128)(2,1)S(1)}, u32[]{:S(2)}, u32[]{:S(2)}) collective-permute-start(bf16[72,4096]{1,0:T(8,128)(2,1)S(1)} %get-tuple-element.7), channel_id=1, source_target_pairs={{0,1},{1,2},{2,3},{3,4},{4,5},{5,6},{6,7},{7,8},{8,9},{9,10},{10,1... | collective-permute-start | bytes 1769480 | tf_op jit(solution)/shard_map/ppermute | solution.py:182
  11.6 28.4 %collective-permute-start.1 = (bf16[72,4096]{1,0:T(8,128)(2,1)S(1)}, bf16[72,4096]{1,0:T(8,128)(2,1)S(1)}, u32[]{:S(2)}, u32[]{:S(2)}) collective-permute-start(bf16[72,4096]{1,0:T(8,128)(2,1)S(1)} %get-tuple-element.6), channel_id=1, source_target_pairs={{1,0},{2,1},{3,2},{4,3},{5,4},{6,5},{7,6},{8,7},{9,8},{10,9},{11,1... | collective-permute-start | bytes 1769480 | tf_op jit(solution)/shard_map/ppermute | solution.py:183
  16.5 0.5 copy-start.4
  46.0 19.1 %all-to-all-start.1 = ((bf16[32,72,128]{2,1,0:T(8,128)(2,1)}), bf16[32,72,128]{2,1,0:T(8,128)(2,1)S(1)}, u32[]{:S(2)}, u32[]{:S(2)}) async-start(bf16[32,72,128]{2,1,0:T(8,128)(2,1)} %halo_tiles.1), calls=%async_computation.1 | async-start | bytes 1179648 | tf_op jit(solution)/shard_map/all_to_all | solution.py:241
  49.6 15.5 %copy-start.1 = (f32[1024]{0:T(1024)S(1)}, f32[1024]{0:T(1024)}, u32[]{:S(2)}) copy-start(f32[1024]{0:T(1024)} %param.15) | copy-start | bytes 12292
